TPU v7x, 256 devices: a whole 4x4x8 slice. The times are simulated.
256 devices in a mesh: shard: 32 (over x, y, core), tensor: 8 (over z).
Axes of the slice: x: 4, y: 4, z: 8, core: 2. Of those that a mesh axis runs over, the one named last changes fastest.
Arguments:
- cand_rows: bfloat16 [65536, 1024], P('shard'), may hold values from -24 to 24
- proj_weight: bfloat16 [1024, 4, 1024], P(None, None, 'tensor'), may hold values from -0.1875 to 0.1875
- out_weight: bfloat16 [1024, 1024], P('tensor'), may hold values from -0.5 to 0.5
- self_bias: float32 [16], P('tensor'), may hold values from 1 to 4
- history_cache: bfloat16 [64, 2048, 2, 1024], P('shard', None, None, 'tensor'), may hold values from -6 to 6
- history_length: int32 [64], replicated, may hold values from 1 to 2048, 65536 in all
- candidate_slot: int32 [65536, 1], P('shard'), may hold values from 0 to 63; in each aligned block of 2048 rows (0 to 2047, 2048 to 4095, ...) at most 64 rows name the same one
- hot_slot: int32 [32], replicated, may hold values from 0 to 1
Outputs:
- layer_out: bfloat16 [65536, 1024], P('shard', 'tensor')
Inputs may be any that keep to these rules, and one draw needn't show every extreme that they name: `candidate_slot`: every cache slot is named by some row; within the rows of one shard index no slot is named more than 64 times, and some shard index names some slot exactly 64 times.
All inputs are finite; a program needn't handle non-finite values.
Results may differ from a plain program's by a relative error of at most 0.0062.
Values may be sent and summed in bfloat16 or wider, within the bound.
No kernel may reach another device: no remote copies, remote signals or barrier semaphores. Data moves between devices by JAX's collectives and lax.ppermute only.
A program may use at most 64 MiB of HBM per device.

v0:
```python
import jax
import jax.numpy as jnp
from jax import lax
from jax.sharding import PartitionSpec as P

DH = 64
HMAX = 2048
KBLK = 512


epsilon = 1e-06


def partner(array, axis, apart):
    return lax.ppermute(array, axis, [(i, i ^ 1 << apart) for i in range(lax.axis_size(axis))])


def attend_rows(packet, cache_slab, length, head_bias, block_count):
    row_count = packet.shape[0]
    head_count = head_bias.shape[0]
    pieces = packet.reshape(row_count, 3, head_count, DH)
    candidate_value = pieces[:, 0]
    query_rows = pieces[:, 1]
    key_self = pieces[:, 2]
    score_scale = DH ** (-0.5)

    def add_block(block_index, running):
        offset = block_index * KBLK
        key_block = lax.dynamic_slice_in_dim(cache_slab, offset, KBLK, 0)
        history_key_rows = key_block[:, 0].reshape(KBLK, head_count, DH)
        history_value_rows = key_block[:, 1].reshape(KBLK, head_count, DH)
        scores = (
            jnp.einsum(
                "wpi,npi->wpn", query_rows, history_key_rows, preferred_element_type=jnp.float32
            )
            * score_scale
        )
        where_live = offset + jnp.arange(KBLK, dtype=jnp.int32) < length
        weight_matrices = jnp.where(where_live[None, None, :], jax.nn.silu(scores), 0.0).astype(
            jnp.bfloat16
        )
        return running + jnp.einsum(
            "jbu,ubl->jbl", weight_matrices, history_value_rows, preferred_element_type=jnp.float32
        )

    initial = jnp.zeros((row_count, head_count, DH), jnp.float32)
    history = lax.fori_loop(0, block_count, add_block, initial)
    self_score = (
        jnp.sum(query_rows.astype(jnp.float32) * key_self.astype(jnp.float32), axis=-1)
        * score_scale
        + head_bias[None, :]
    )
    merged = history + jax.nn.silu(self_score)[..., None] * candidate_value.astype(jnp.float32)
    return merged.astype(jnp.bfloat16).reshape(row_count, head_count * DH)


def body(
    cand_rows,
    proj_weight,
    out_weight,
    self_bias,
    history_cache,
    history_length,
    candidate_slot,
    hot_slot,
):
    shard_count = lax.axis_size("shard")
    my_shard = lax.axis_index("shard")
    tensor_count = lax.axis_size("tensor")
    my_tensor = lax.axis_index("tensor")
    row_count, model_width = cand_rows.shape
    local_width = out_weight.shape[0]
    slot_count = history_cache.shape[0]
    slot_total = shard_count * slot_count
    capacity = 2 * row_count // slot_total
    half_axis = shard_count // 2
    partner_bit = half_axis.bit_length() - 1
    mean_square = jnp.mean(jnp.square(cand_rows.astype(jnp.float32)), axis=1, keepdims=True)
    projected = jnp.dot(
        cand_rows,
        proj_weight.reshape(model_width, 4 * local_width),
        preferred_element_type=jnp.float32,
    )
    projected = jax.nn.silu(projected / jnp.sqrt(mean_square + epsilon)).astype(jnp.bfloat16)
    projected = projected.reshape(row_count, 4, local_width)
    gate_rows = projected[:, 0]
    packets = projected[:, 1:].reshape(row_count, 3 * local_width)
    slot_ids = candidate_slot[:, 0]
    own_lengths = lax.dynamic_slice_in_dim(history_length, my_shard * slot_count, slot_count)
    my_hot = lax.dynamic_index_in_dim(hot_slot, my_shard, 0, keepdims=False)
    partner_shard = jnp.bitwise_xor(my_shard, half_axis)
    their_hot = lax.dynamic_index_in_dim(hot_slot, partner_shard, 0, keepdims=False)
    outgoing = lax.dynamic_index_in_dim(history_cache, my_hot, 0, keepdims=False)
    arriving_rows = partner(outgoing, "shard", partner_bit)
    local_cache = lax.dynamic_update_index_in_dim(history_cache, arriving_rows, my_hot, 0)
    moved_length = lax.dynamic_index_in_dim(
        history_length, partner_shard * slot_count + their_hot, 0, keepdims=False
    )
    local_lengths = own_lengths.at[my_hot].set(moved_length)
    matches = (slot_ids[:, None] == jnp.arange(slot_total, dtype=jnp.int32)[None, :]).astype(
        jnp.int32
    )
    ranks = jnp.sum(jnp.cumsum(matches, axis=0) * matches, axis=1) - 1
    positions = slot_ids * capacity + ranks
    outbound = (
        jnp.zeros((slot_total * capacity, 3 * local_width), jnp.bfloat16).at[positions].set(packets)
    )
    outbound = outbound.reshape(shard_count, slot_count, capacity, 3 * local_width)
    received = lax.all_to_all(outbound, "shard", split_axis=0, concat_axis=0, tiled=True)
    item_count = received.shape[2]
    answers = []
    for slot_index in range(slot_count):
        rows_here = received[:, slot_index].reshape(shard_count * item_count, 3 * local_width)
        length = local_lengths[slot_index]
        block_count = HMAX // KBLK
        answer = attend_rows(rows_here, local_cache[slot_index], length, self_bias, block_count)
        answers.append(answer.reshape(shard_count, item_count, local_width))
    answered = jnp.stack(answers, axis=1)
    returned = lax.all_to_all(answered, "shard", split_axis=0, concat_axis=0, tiled=True)
    attention = returned.reshape(slot_total * capacity, local_width)[positions]
    attn_wide = attention.astype(jnp.float32).reshape(row_count, local_width // DH, DH)
    normed = attn_wide / jnp.sqrt(jnp.mean(attn_wide * attn_wide, axis=-1, keepdims=True) + epsilon)
    hidden = (normed.reshape(row_count, local_width) * gate_rows.astype(jnp.float32)).astype(
        jnp.bfloat16
    )
    column_count = model_width // tensor_count
    residual = lax.dynamic_slice_in_dim(
        cand_rows, my_tensor * column_count, column_count, 1
    ).astype(jnp.float32)
    partial_sum = jnp.dot(hidden, out_weight, preferred_element_type=jnp.float32)
    mixed = lax.psum_scatter(partial_sum, "tensor", scatter_dimension=1, tiled=True)
    return (residual + mixed).astype(jnp.bfloat16)


def solution(mesh):
    in_specs = (
        P("shard", None),
        P(None, None, "tensor"),
        P("tensor", None),
        P("tensor"),
        P("shard", None, None, "tensor"),
        P(),
        P("shard", None),
        P(),
    )
    out_specs = P("shard", "tensor")
    return jax.shard_map(body, mesh=mesh, in_specs=in_specs, out_specs=out_specs, check_vma=False)
```

profile of v0, /device:TPU:1, one launch (start us, length us, event | category | flops | bytes accessed | tf_op | source)
XLA Modules:
  0.0 354.2 jit_solution(11683907771234707169)
XLA Ops:
  6.5 3.2 multiply_reduce_fusion
  9.8 18.1 %reduce-window.6 = s32[64,16,128]{2,1,0:T(8,128)S(1)} reduce-window(s32[64,16,128]{2,1,0:T(8,128)S(1)} %fusion.35, s32[]{:T(128)} %constant.171.clone.1), window={size=1x1x128 pad=0_0x0_0x127_0}, to_apply=%region_0.0 | reduce-window | flops 16646144 | bytes 1048580 | tf_op jit(solution)/shard_map/reduce-window
  29.2 5.4 %multiply_convert_fusion = bf16[2048,512]{0,1:T(8,128)(2,1)S(1)} fusion(bf16[2048,1024]{1,0:T(8,128)(2,1)} %param.14, f32[2048]{0:T(1024)S(1)} %add_sqrt_fusion.1, bf16[128,8,4,128]{3,2,1,0:T(4,128)(2,1)S(1)} %bitcast.177), kind=kOutput, calls=%fused_computation.33 | convolution fusion | flops 2153775104 | bytes 7348224 | tf_op jit(solution)/shard_map/dot_general | solution.py:79
  34.6 1.3 copy-done.2
  36.0 0.9 copy.48
  36.9 11.6 %scatter_custom_fusion = bf16[4096,384]{1,0:T(8,128)(2,1)} fusion(s32[2048]{0:T(1024)S(1)} %bitcast.174, bf16[2048,384]{1,0:T(8,128)(2,1)S(1)} %copy.48, bf16[]{:T(256)} %constant.180.clone.1), kind=kCustom, calls=%fused_computation.35 | custom fusion | bytes 3145730 | tf_op jit(solution)/shard_map/scatter | solution.py:106
  48.5 8.6 %all-to-all-start = ((bf16[32,2,64,384]{3,2,1,0:T(8,128)(2,1)}), bf16[32,2,64,384]{3,2,1,0:T(8,128)(2,1)S(1)}, u32[]{:S(2)}, u32[]{:S(2)}) async-start(bf16[32,2,64,384]{3,2,1,0:T(8,128)(2,1)} %bitcast.157), calls=%async_computation | async-start | bytes 6291456 | tf_op jit(solution)/shard_map/all_to_all | solution.py:109
  57.1 0.6 fusion.40
  59.4 2.6 constant_dynamic-slice_fusion.4
  62.0 3.7 %copy.44 = bf16[1,2048,2,128]{1,3,2,0:T(8,128)(2,1)} copy(bf16[1,2048,2,128]{3,2,1,0:T(2,128)(2,1)} %constant_dynamic-slice_fusion.4) | data formatting | bytes 2097152 | tf_op jit(solution)/shard_map/jit(dynamic_index_in_dim)/dynamic_slice | solution.py:93
  65.7 2.9 collective-permute-start
  69.3 6.2 %copy.45 = bf16[2,2048,2,128]{1,3,2,0:T(8,128)(2,1)} copy(bf16[2,2048,2,128]{3,2,1,0:T(2,128)(2,1)} %param.18) | data formatting | bytes 4194304 | tf_op args[4]
  76.4 42.6 %collective-permute-done = bf16[2048,2,128]{0,2,1:T(8,128)(2,1)} collective-permute-done((bf16[2048,2,128]{0,2,1:T(8,128)(2,1)}, bf16[2048,2,128]{0,2,1:T(8,128)(2,1)}, u32[]{:S(2)}, u32[]{:S(2)}) %collective-permute-start) | collective-permute-done | bytes 1048608 | tf_op jit(solution)/shard_map/ppermute | solution.py:15
  119.0 2.3 bitcast_dynamic-update-slice_fusion
  121.3 3.1 slice_bitcast_fusion.1
  124.4 2.0 fusion.37
  126.4 5.5 %reshape.180 = bf16[2048,3,2,64]{3,2,1,0:T(2,128)(2,1)S(1)} reshape(bf16[32,1,64,384]{3,2,1,0:T(8,128)(2,1)} %get-tuple-element.270) | data formatting | bytes 3145728 | tf_op jit(solution)/shard_map/reshape;reshape;squeeze | solution.py:21
  132.0 3.2 fusion.36
  135.2 2.5 copy.61
  137.7 2.4 copy.60
  140.1 3.5 copy.62
  143.8 20.6 %while.29 = (s32[]{:T(128)}, f32[2048,2,64]{0,2,1:T(8,128)S(1)}, bf16[2048,2,128]{0,2,1:T(8,128)(2,1)}, s32[]{:T(128)}, bf16[2048,2,64]{0,2,1:T(8,128)(2,1)S(1)}...) while((s32[]{:T(128)}, f32[2048,2,64]{0,2,1:T(8,128)S(1)}, ...), condition=%wide.region_6.7_spmd.clone, body=%wide.region_5.6_spmd.clone.sunk | while | flops 552076288 | bytes 3409089 | solution.py:47
  143.8 0.6 add_compare_fusion.4
  144.4 1.0 constant_dynamic-slice_fusion.7
  145.4 3.5 fusion.60
  148.9 0.6 add_compare_fusion.4
  149.6 1.0 constant_dynamic-slice_fusion.7
  150.6 3.5 fusion.60
  154.1 0.6 add_compare_fusion.4
  154.7 1.0 constant_dynamic-slice_fusion.7
  155.7 3.5 fusion.60
  159.2 0.6 add_compare_fusion.4
  159.9 1.0 constant_dynamic-slice_fusion.7
  160.9 3.5 fusion.60
  164.4 1.0 copy-done.5
  165.3 5.5 %reshape.181 = bf16[2048,3,2,64]{3,2,1,0:T(2,128)(2,1)S(1)} reshape(bf16[32,1,64,384]{3,2,1,0:T(8,128)(2,1)} %get-tuple-element.271) | data formatting | bytes 3145728 | tf_op jit(solution)/shard_map/reshape;reshape;squeeze | solution.py:21
  170.9 3.2 fusion.38
  174.1 2.4 copy.64
  176.5 2.4 copy.63
  179.1 27.7 %while.30 = (s32[]{:T(128)}, f32[2048,2,64]{0,2,1:T(8,128)}, bf16[2048,2,128]{0,2,1:T(8,128)(2,1)}, s32[]{:T(128)}, bf16[2048,2,64]{0,2,1:T(8,128)(2,1)S(1)}, /*...) while((s32[]{:T(128)}, f32[2048,2,64]{0,2,1:T(8,128)}, bf16[2048,2,128]{0,2,1:T(8,128)(2,1)}, ...), condition=%wide.region_9.10_spmd.clone, body=%wide.region_8.9_spmd.clone.sunk | while | flops 552076288 | bytes 3409089 | solution.py:47
  179.3 0.7 add_compare_fusion.5
  180.1 1.0 constant_dynamic-slice_fusion.8
  181.1 4.3 %fusion.64 = f32[2048,2,64]{0,2,1:T(8,128)} fusion(bf16[512,2,64]{0,2,1:T(8,128)(2,1)S(1)} %bitcast.163, bf16[512,2,64]{0,2,1:T(8,128)(2,1)S(1)} %bitcast.162, bf16[2048,2,64]{0,2,1:T(8,128)(2,1)S(1)} %get-tuple-element.379, pred[512]{0:T(512)(128)(4,1)S(1)} %add_compare_fusion.5, f32[2048,2,64]{0,2,1:T(8,128)} %get-tuple-element.366, pred[]{:T(512)S(6)} %compare.20), kind=kOutput, calls=%fused_computation.25.clone.1 | convolution fusion | flops 552075264 | bytes 2884097 | tf_op jit(solution)/shard_map/while/body/eval_jaxpr/jbu,ubl->jbl/dot_general | solution.py:42
  185.4 0.6 add_compare_fusion.5
  186.0 1.0 constant_dynamic-slice_fusion.8
  187.0 5.6 %fusion.64 = f32[2048,2,64]{0,2,1:T(8,128)} fusion(bf16[512,2,64]{0,2,1:T(8,128)(2,1)S(1)} %bitcast.163, bf16[512,2,64]{0,2,1:T(8,128)(2,1)S(1)} %bitcast.162, bf16[2048,2,64]{0,2,1:T(8,128)(2,1)S(1)} %get-tuple-element.379, pred[512]{0:T(512)(128)(4,1)S(1)} %add_compare_fusion.5, f32[2048,2,64]{0,2,1:T(8,128)} %get-tuple-element.366, pred[]{:T(512)S(6)} %compare.20), kind=kOutput, calls=%fused_computation.25.clone.1 | convolution fusion | flops 552075264 | bytes 2884097 | tf_op jit(solution)/shard_map/while/body/eval_jaxpr/jbu,ubl->jbl/dot_general | solution.py:42
  192.5 0.6 add_compare_fusion.5
  193.1 1.0 constant_dynamic-slice_fusion.8
  194.1 5.6 %fusion.64 = f32[2048,2,64]{0,2,1:T(8,128)} fusion(bf16[512,2,64]{0,2,1:T(8,128)(2,1)S(1)} %bitcast.163, bf16[512,2,64]{0,2,1:T(8,128)(2,1)S(1)} %bitcast.162, bf16[2048,2,64]{0,2,1:T(8,128)(2,1)S(1)} %get-tuple-element.379, pred[512]{0:T(512)(128)(4,1)S(1)} %add_compare_fusion.5, f32[2048,2,64]{0,2,1:T(8,128)} %get-tuple-element.366, pred[]{:T(512)S(6)} %compare.20), kind=kOutput, calls=%fused_computation.25.clone.1 | convolution fusion | flops 552075264 | bytes 2884097 | tf_op jit(solution)/shard_map/while/body/eval_jaxpr/jbu,ubl->jbl/dot_general | solution.py:42
  200.2 1.0 constant_dynamic-slice_fusion.8
  201.2 5.6 %fusion.64 = f32[2048,2,64]{0,2,1:T(8,128)} fusion(bf16[512,2,64]{0,2,1:T(8,128)(2,1)S(1)} %bitcast.163, bf16[512,2,64]{0,2,1:T(8,128)(2,1)S(1)} %bitcast.162, bf16[2048,2,64]{0,2,1:T(8,128)(2,1)S(1)} %get-tuple-element.379, pred[512]{0:T(512)(128)(4,1)S(1)} %add_compare_fusion.5, f32[2048,2,64]{0,2,1:T(8,128)} %get-tuple-element.366, pred[]{:T(512)S(6)} %compare.20), kind=kOutput, calls=%fused_computation.25.clone.1 | convolution fusion | flops 552075264 | bytes 2884097 | tf_op jit(solution)/shard_map/while/body/eval_jaxpr/jbu,ubl->jbl/dot_general | solution.py:42
  206.8 0.7 copy.65
  207.7 1.8 fusion.25
  209.5 1.1 stack_reshape_reshape.7
  210.6 2.0 stack_reshape_reshape.6
  212.7 1.7 pad_maximum_fusion
  214.4 2.5 copy.51
  216.8 5.4 %all-to-all-start.1 = ((bf16[32,2,64,128]{3,2,1,0:T(8,128)(2,1)}), bf16[32,2,64,128]{3,2,1,0:T(8,128)(2,1)S(1)}, u32[]{:S(2)}, u32[]{:S(2)}) async-start(bf16[32,2,64,128]{3,2,1,0:T(8,128)(2,1)} %copy.51), calls=%async_computation.1 | async-start | bytes 2097152 | tf_op jit(solution)/shard_map/all_to_all | solution.py:119
  222.3 1.1 slice.120
  223.7 15.5 %all-to-all-done.1 = bf16[32,2,64,128]{3,2,1,0:T(8,128)(2,1)S(1)} async-done(((bf16[32,2,64,128]{3,2,1,0:T(8,128)(2,1)}), bf16[32,2,64,128]{3,2,1,0:T(8,128)(2,1)S(1)}, u32[]{:S(2)}, u32[]{:S(2)}) %all-to-all-start.1) | async-done | bytes 1048608 | tf_op jit(solution)/shard_map/all_to_all | solution.py:119
  239.2 6.2 %gather_fusion = bf16[2048,128]{1,0:T(8,128)(2,1)S(1)} fusion(bf16[4096,128]{1,0:T(8,128)(2,1)S(1)} %bitcast.156, s32[2048]{0:T(1024)S(1)} %broadcast_clamp_fusion), kind=kCustom, calls=%fused_computation | custom fusion | bytes 1056768 | tf_op jit(solution)/shard_map/gather | solution.py:120
  246.4 4.5 %fusion.30 = f32[2048,1024]{1,0:T(8,128)} fusion(bf16[128,1024]{1,0:T(8,128)(2,1)S(1)} %copy-done, f32[2048,128]{1,0:T(8,128)S(1)} %copy.53, bf16[2048,128]{1,0:T(8,128)(2,1)S(1)} %gather_fusion, bf16[2048,1,128]{2,0,1:T(8,128)(2,1)S(1)} %copy.66), kind=kOutput, calls=%fused_computation.58 | convolution fusion | flops 538181632 | bytes 10747904 | tf_op jit(solution)/shard_map/dot_general | solution.py:130
  250.9 94.3 %reduce-scatter.2.cloned.1.call-done = f32[2048,128]{1,0:T(8,128)} async-done(((f32[2048,1024]{1,0:T(8,128)}), f32[2048,128]{1,0:T(8,128)}) %reduce-scatter.2.cloned.1.call-update) | async-done | bytes 1048592 | tf_op jit(solution)/shard_map/reduce_scatter | solution.py:131
  345.1 2.3 add_convert_fusion
  (50 shorter events, 4.6 us)
Async XLA Ops:
  6.5 239.8 %copy-start = (bf16[128,1024]{1,0:T(8,128)(2,1)S(1)}, bf16[128,1024]{1,0:T(8,128)(2,1)}, u32[]{:S(2)}) copy-start(bf16[128,1024]{1,0:T(8,128)(2,1)} %param.16) | copy-start | bytes 786436
  6.5 3.2 copy-start.6
  6.5 22.7 %copy-start.10 = (bf16[1024,4,128]{2,1,0:T(4,128)(2,1)S(1)}, bf16[1024,4,128]{2,1,0:T(4,128)(2,1)}, u32[]{:S(2)}) copy-start(bf16[1024,4,128]{2,1,0:T(4,128)(2,1)} %param.15) | copy-start | bytes 3145732
  34.6 1.3 copy-start.2
  36.9 20.2 %copy-start.7 = (s32[32]{0:T(128)S(1)}, s32[32]{0:T(128)}, u32[]{:S(2)}) copy-start(s32[32]{0:T(128)} %param.21) | copy-start | bytes 388
  48.5 75.9 %all-to-all-start = ((bf16[32,2,64,384]{3,2,1,0:T(8,128)(2,1)}), bf16[32,2,64,384]{3,2,1,0:T(8,128)(2,1)S(1)}, u32[]{:S(2)}, u32[]{:S(2)}) async-start(bf16[32,2,64,384]{3,2,1,0:T(8,128)(2,1)} %bitcast.157), calls=%async_computation | async-start | bytes 6291456 | tf_op jit(solution)/shard_map/all_to_all | solution.py:109
  59.4 16.1 %copy-start.8 = (s32[64]{0:T(128)S(1)}, s32[64]{0:T(128)}, u32[]{:S(2)}) copy-start(s32[64]{0:T(128)} %param.19) | copy-start | bytes 772
  65.7 53.2 %collective-permute-start = (bf16[2048,2,128]{0,2,1:T(8,128)(2,1)}, bf16[2048,2,128]{0,2,1:T(8,128)(2,1)}, u32[]{:S(2)}, u32[]{:S(2)}) collective-permute-start(bf16[2048,2,128]{0,2,1:T(8,128)(2,1)} %bitcast.169), channel_id=1, source_target_pairs={{0,128},{8,136},{16,144},{24,152},{32,160},{40,168},{48,176},{56,1... | collective-permute-start | bytes 3145736 | tf_op jit(solution)/shard_map/ppermute | solution.py:15
  135.2 8.6 %copy-start.4 = (f32[2048,2,64]{0,2,1:T(8,128)S(1)}, f32[2048,2,64]{0,2,1:T(8,128)}, u32[]{:S(2)}) copy-start(f32[2048,2,64]{0,2,1:T(8,128)} %custom-call) | copy-start | bytes 3145732
  164.4 1.0 copy-start.5
  179.1 27.7 %copy-start.1 = (bf16[2048,1,2,64]{3,2,1,0:T(2,128)(2,1)S(1)}, bf16[2048,1,2,64]{3,2,1,0:T(2,128)(2,1)}, u32[]{:S(2)}) copy-start(bf16[2048,1,2,64]{3,2,1,0:T(2,128)(2,1)} %get-tuple-element.274) | copy-start | bytes 1572868
  179.1 28.5 %copy-start.9 = (f32[2]{0:T(128)S(1)}, f32[2]{0:T(128)}, u32[]{:S(2)}) copy-start(f32[2]{0:T(128)} %param.17) | copy-start | bytes 28
  179.1 28.6 %copy-start.3 = (bf16[2048,1,2,64]{0,3,2,1:T(8,128)(2,1)S(1)}, bf16[2048,1,2,64]{0,3,2,1:T(8,128)(2,1)}, u32[]{:S(2)}) copy-start(bf16[2048,1,2,64]{0,3,2,1:T(8,128)(2,1)} %copy.62) | copy-start | bytes 1572868
  216.8 22.4 %all-to-all-start.1 = ((bf16[32,2,64,128]{3,2,1,0:T(8,128)(2,1)}), bf16[32,2,64,128]{3,2,1,0:T(8,128)(2,1)S(1)}, u32[]{:S(2)}, u32[]{:S(2)}) async-start(bf16[32,2,64,128]{3,2,1,0:T(8,128)(2,1)} %copy.51), calls=%async_computation.1 | async-start | bytes 2097152 | tf_op jit(solution)/shard_map/all_to_all | solution.py:119
  222.3 122.8 %reduce-scatter.2.cloned.1.call-start = ((), (), s32[]{:S(2)}) async-start(), calls=%async_computation.3 | async-start | bytes 9437184 | tf_op jit(solution)/shard_map/reduce_scatter | solution.py:131
Sparse Core Ops, SparseCore 0:
  251.0 94.1 reduce-scatter.1
where the time goes:
time: 356 us; the launch traced here: 354 us
  waiting for transfers between devices  152 us (43%)
  local copies, waits for them, and re-layouts  90 us (25%)
  matrix products  44.8 us (13%)
  other arithmetic  33.6 us (9%)
  starting transfers between devices  17 us (5%)
  between operations  16.2 us (5%)
    reduce_scatter x1, waiting for transfers between devices, body(): lax.psum_scatter(partial_sum, 'tensor', scatter_dimension=1, tiled=True)  94.3 us
    ppermute x1, waiting for transfers between devices, partner(): lax.ppermute(array, axis, [(i, i ^ 1 << apart) for i in range(lax.axis_si...  42.6 us
    dot_general x8, matrix products, add_block(): jnp.einsum('jbu,ubl->jbl', weight_matrices, history_value_rows, preferred...  34.9 us
    unnamed x30, local copies, waits for them, and re-layouts  22.7 us
    another operation x3, other arithmetic  18.5 us
    all_to_all x1, waiting for transfers between devices, body(): lax.all_to_all(answered, 'shard', split_axis=0, concat_axis=0, tiled=True)  15.5 us
    scatter x1, local copies, waits for them, and re-layouts, body(): jnp.zeros((slot_total * capacity, 3 * local_width), jnp.bfloat16)  11.6 us
    another operation x2, local copies, waits for them, and re-layouts, attend_rows(): pieces = packet.reshape(row_count, 3, head_count, DH)  11.1 us
  transfers between devices with their start and end apart: 4, of which 3 were waited for; matrix products, arithmetic and copies ran while one was open for 6% of the time, Pallas kernels for 0%

commit v1 on v0

v1 whole, which is shorter than its diff:
```python
import functools

import jax
import jax.numpy as jnp
from jax import lax
from jax.experimental import pallas as pl
from jax.experimental.pallas import tpu as pltpu
from jax.sharding import PartitionSpec as P

DH = 64
epsilon = 1e-06
BF = jnp.bfloat16
F32 = jnp.float32
ROWS = 256
SCATTER = 512
KBLK = 512
VMEM_LIMIT = 48 * 1024 * 1024


def dot(a, b):
    return jnp.dot(a, b, preferred_element_type=F32)


def inverse_rms(rows):
    wide = rows.astype(F32)
    return lax.rsqrt(jnp.mean(wide * wide, axis=1, keepdims=True) + epsilon)


def silu(x):
    half = 0.5 * x
    return half + half * jnp.tanh(half)


def query_kernel(capacity, cand_ref, weight_ref, slot_ref, source_ref, sent_ref, query_ref, key_ref, queries, keys, carry):
    step = pl.program_id(0)
    slot_total = source_ref.shape[0]
    column = source_ref[...].astype(F32) * capacity - 1.0

    @pl.when(step == 0)
    def _():
        carry[...] = jnp.zeros_like(carry)

    rows = cand_ref[...]
    query = silu(dot(rows, weight_ref[...]) * inverse_rms(rows)).astype(BF) * BF(0.5 * DH**-0.5)
    query_ref[...] = query
    start = pl.multiple_of(step * ROWS, ROWS)
    queries[pl.ds(start, ROWS), :] = query

    slots = slot_ref[:, pl.ds(start, ROWS)]
    member = (slots == lax.broadcasted_iota(jnp.int32, (slot_total, ROWS), 0)).astype(F32)
    before = lax.broadcasted_iota(jnp.int32, (ROWS, ROWS), 0) <= lax.broadcasted_iota(jnp.int32, (ROWS, ROWS), 1)
    counted = dot(member.astype(BF), before.astype(BF)) + carry[:, :1]
    carry[...] = jnp.broadcast_to(counted[:, ROWS - 1 :], carry.shape)
    keys[:, pl.ds(start, ROWS)] = jnp.sum(member * (counted + column), axis=0, keepdims=True).astype(jnp.int32)

    @pl.when(step == pl.num_programs(0) - 1)
    def _():
        key_ref[...] = keys[...]

        @pl.loop(0, slot_total * capacity // SCATTER)
        def _(block):
            per = SCATTER // capacity
            lane_keys = keys[...]
            local = lax.broadcasted_iota(jnp.int32, (capacity, lane_keys.shape[1]), 0)
            parts = [
                (lane_keys - (block * per + i) * capacity == local).astype(F32).astype(BF)
                for i in range(per)
            ]
            picked = dot(jnp.concatenate(parts, axis=0), queries[...])
            sent_ref[pl.ds(pl.multiple_of(block * SCATTER, SCATTER), SCATTER), :] = picked.astype(BF)


def side_kernel(cand_ref, weight_ref, query_ref, bias_ref, gate_ref, self_ref):
    rows = cand_ref[...]
    width = gate_ref.shape[1]
    parts = silu(dot(rows, weight_ref[...]) * inverse_rms(rows)).astype(BF)
    gate_ref[...] = parts[:, :width]
    value = parts[:, width : 2 * width].astype(F32)
    product = query_ref[...].astype(F32) * parts[:, 2 * width :].astype(F32)
    lane = lax.broadcasted_iota(jnp.int32, product.shape, 1)
    score = jnp.zeros_like(product)
    for head in range(width // DH):
        here = lane // DH == head
        total = jnp.sum(jnp.where(here, product, 0.0), axis=1, keepdims=True)
        score = jnp.where(here, 2.0 * total + bias_ref[head], score)
    self_ref[...] = silu(score) * value


def attend_kernel(length_ref, packet_ref, key_ref, value_ref, answer_ref, masked):
    shard_count, slot_count, item_count, width = packet_ref.shape
    heads = width // DH
    history = key_ref.shape[2]
    group = ROWS // item_count
    for slot in range(slot_count):
        length = length_ref[slot]
        blocks = (length + KBLK - 1) // KBLK
        lane = lax.broadcasted_iota(jnp.int32, (KBLK, width), 1)

        @pl.loop(0, blocks)
        def _(block):
            offset = pl.multiple_of(block * KBLK, KBLK)
            values = value_ref[slot, pl.ds(offset, KBLK), :]
            live = offset + lax.broadcasted_iota(jnp.int32, (KBLK, width), 0) < length
            for head in range(heads):
                masked[block, head * KBLK : (head + 1) * KBLK, :] = jnp.where(
                    live & (lane // DH == head), values.astype(F32), 0.0
                ).astype(BF)

        @pl.loop(0, shard_count // group)
        def _(part):
            rows = packet_ref[pl.ds(part * group, group), slot].reshape(ROWS, width)
            row_lane = lax.broadcasted_iota(jnp.int32, (ROWS, width), 1)
            stacked = jnp.concatenate(
                [jnp.where(row_lane // DH == head, rows.astype(F32), 0.0).astype(BF) for head in range(heads)], axis=0
            )

            def add_block(block, total):
                offset = pl.multiple_of(block * KBLK, KBLK)
                half = dot(stacked, key_ref[slot, :, pl.ds(offset, KBLK)])
                weights = (half + half * jnp.tanh(half)).astype(BF)
                wide = jnp.concatenate([weights[head * ROWS : (head + 1) * ROWS] for head in range(heads)], axis=1)
                return total + dot(wide, masked[block])

            total = lax.fori_loop(0, blocks, add_block, jnp.zeros((ROWS, width), F32))
            answer_ref[pl.ds(part * group, group), slot] = total.astype(BF).reshape(group, item_count, width)


def hidden_kernel(key_ref, returned_ref, self_ref, gate_ref, hidden_ref):
    rows, width = gate_ref.shape
    positions = returned_ref.shape[0]
    chosen = (key_ref[...] == lax.broadcasted_iota(jnp.int32, (rows, positions), 1)).astype(F32).astype(BF)
    attention = dot(chosen, returned_ref[...]) + self_ref[...]
    square = attention * attention
    high = square.astype(BF)
    low = (square - high.astype(F32)).astype(BF)
    same = (
        lax.broadcasted_iota(jnp.int32, (width, width), 0) // DH
        == lax.broadcasted_iota(jnp.int32, (width, width), 1) // DH
    )
    ones = same.astype(F32).astype(BF)
    mean = (dot(high, ones) + dot(low, ones)) * (1.0 / DH)
    hidden_ref[...] = (attention * lax.rsqrt(mean + epsilon) * gate_ref[...].astype(F32)).astype(BF)


def output_kernel(place_ref, hidden_ref, weight_ref, residual_ref, out_ref):
    hidden = jnp.concatenate([hidden_ref[i] for i in range(hidden_ref.shape[0])], axis=1)
    mixed = (residual_ref[...].astype(F32) + dot(hidden, weight_ref[...])).astype(BF)
    part = out_ref.shape[2]
    for i in range(out_ref.shape[0]):
        out_ref[i] = mixed[:, i * part : (i + 1) * part]


def params(**more):
    return pltpu.CompilerParams(vmem_limit_bytes=VMEM_LIMIT, **more)


def body(cand_rows, proj_weight, out_weight, self_bias, history_cache, history_length, candidate_slot, hot_slot):
    shard_count = lax.axis_size("shard")
    my_shard = lax.axis_index("shard")
    tensor_count = lax.axis_size("tensor")
    my_tensor = lax.axis_index("tensor")
    row_count, model_width = cand_rows.shape
    width = out_weight.shape[0]
    slot_count = history_cache.shape[0]
    slot_total = shard_count * slot_count
    capacity = 2 * row_count // slot_total
    history = history_cache.shape[1]
    positions = slot_total * capacity
    steps = row_count // ROWS

    shards = jnp.arange(shard_count, dtype=jnp.int32)
    others = shards ^ (shard_count // 2)
    partner_hot = jnp.concatenate([hot_slot[shard_count // 2 :], hot_slot[: shard_count // 2]])
    local = jnp.arange(slot_count, dtype=jnp.int32)
    named = shards[:, None] * slot_count + local[None, :]
    sources = jnp.where(
        local[None, :] == hot_slot[:, None], (others * slot_count + partner_hot)[:, None], named
    ).reshape(slot_total, 1)

    full_weight = lax.all_gather(out_weight, "tensor", axis=0, tiled=True)

    query_weight = proj_weight[:, 2, :]
    slot_row = candidate_slot.reshape(1, row_count)
    sent, queries, keys = pl.pallas_call(
        functools.partial(query_kernel, capacity),
        grid=(steps,),
        in_specs=[
            pl.BlockSpec((ROWS, model_width), lambda i: (i, 0)),
            pl.BlockSpec((model_width, width), lambda i: (0, 0)),
            pl.BlockSpec((1, row_count), lambda i: (0, 0)),
            pl.BlockSpec((slot_total, 1), lambda i: (0, 0)),
        ],
        out_specs=[
            pl.BlockSpec((positions, width), lambda i: (0, 0)),
            pl.BlockSpec((ROWS, width), lambda i: (i, 0)),
            pl.BlockSpec((1, row_count), lambda i: (0, 0)),
        ],
        out_shape=[
            jax.ShapeDtypeStruct((positions, width), BF),
            jax.ShapeDtypeStruct((row_count, width), BF),
            jax.ShapeDtypeStruct((1, row_count), jnp.int32),
        ],
        scratch_shapes=[
            pltpu.VMEM((row_count, width), BF),
            pltpu.VMEM((1, row_count), jnp.int32),
            pltpu.VMEM((slot_total, 128), F32),
        ],
        compiler_params=params(),
        cost_estimate=pl.CostEstimate(flops=4 * 10**9, bytes_accessed=6 * 2**20, transcendentals=2**18),
        name="query",
    )(cand_rows, query_weight, slot_row, sources)

    received = lax.all_to_all(
        sent.reshape(shard_count, slot_count * capacity, width), "shard", split_axis=0, concat_axis=0, tiled=True
    ).reshape(shard_count, slot_count, capacity, width)

    side_weight = jnp.concatenate([proj_weight[:, 0], proj_weight[:, 1], proj_weight[:, 3]], axis=1)
    gate, self_term = pl.pallas_call(
        side_kernel,
        grid=(steps,),
        in_specs=[
            pl.BlockSpec((ROWS, model_width), lambda i: (i, 0)),
            pl.BlockSpec((model_width, 3 * width), lambda i: (0, 0)),
            pl.BlockSpec((ROWS, width), lambda i: (i, 0)),
            pl.BlockSpec(memory_space=pltpu.SMEM),
        ],
        out_specs=[pl.BlockSpec((ROWS, width), lambda i: (i, 0)), pl.BlockSpec((ROWS, width), lambda i: (i, 0))],
        out_shape=[jax.ShapeDtypeStruct((row_count, width), BF), jax.ShapeDtypeStruct((row_count, width), F32)],
        compiler_params=params(),
        cost_estimate=pl.CostEstimate(flops=4 * 10**9, bytes_accessed=6 * 2**20, transcendentals=2**20),
        name="side",
    )(cand_rows, side_weight, queries, self_bias)

    cache_keys = jnp.swapaxes(history_cache[:, :, 0, :], 1, 2)
    cache_values = history_cache[:, :, 1, :]
    key_column = keys.reshape(row_count, 1)
    lengths = lax.dynamic_slice_in_dim(history_length, my_shard * slot_count, slot_count)

    answered = pl.pallas_call(
        attend_kernel,
        in_specs=[pl.BlockSpec(memory_space=pltpu.SMEM)] + [pl.BlockSpec(memory_space=pltpu.VMEM)] * 3,
        out_specs=pl.BlockSpec(memory_space=pltpu.VMEM),
        out_shape=jax.ShapeDtypeStruct(received.shape, BF),
        scratch_shapes=[pltpu.VMEM((history // KBLK, width // DH * KBLK, width), BF)],
        compiler_params=params(),
        cost_estimate=pl.CostEstimate(flops=12 * 10**9, bytes_accessed=4 * 2**20, transcendentals=2**24),
        name="attend",
    )(lengths, received, cache_keys, cache_values)

    returned = lax.all_to_all(
        answered.reshape(shard_count, slot_count * capacity, width), "shard", split_axis=0, concat_axis=0, tiled=True
    ).reshape(positions, width)

    hidden_rows = 512
    hidden = pl.pallas_call(
        hidden_kernel,
        grid=(row_count // hidden_rows,),
        in_specs=[
            pl.BlockSpec((hidden_rows, 1), lambda i: (i, 0)),
            pl.BlockSpec((positions, width), lambda i: (0, 0)),
            pl.BlockSpec((hidden_rows, width), lambda i: (i, 0)),
            pl.BlockSpec((hidden_rows, width), lambda i: (i, 0)),
        ],
        out_specs=pl.BlockSpec((hidden_rows, width), lambda i: (i, 0)),
        out_shape=jax.ShapeDtypeStruct((row_count, width), BF),
        compiler_params=params(),
        cost_estimate=pl.CostEstimate(flops=4 * 10**9, bytes_accessed=4 * 2**20, transcendentals=2**18),
        name="hidden",
    )(key_column, returned, self_term, gate)

    owned = row_count // tensor_count
    gathered = lax.all_to_all(
        hidden.reshape(tensor_count, owned, width), "tensor", split_axis=0, concat_axis=0, tiled=True
    )
    out_width = model_width // tensor_count
    mixed = pl.pallas_call(
        output_kernel,
        grid_spec=pltpu.PrefetchScalarGridSpec(
            num_scalar_prefetch=1,
            grid=(tensor_count // 2,),
            in_specs=[
                pl.BlockSpec((tensor_count, owned, width), lambda i, place: (0, 0, 0)),
                pl.BlockSpec((model_width, 2 * out_width), lambda i, place: (0, i)),
                pl.BlockSpec((owned, 2 * out_width), lambda i, place: (place[0], i)),
            ],
            out_specs=pl.BlockSpec((2, owned, out_width), lambda i, place: (i, 0, 0)),
        ),
        out_shape=jax.ShapeDtypeStruct((tensor_count, owned, out_width), BF),
        compiler_params=params(),
        cost_estimate=pl.CostEstimate(flops=10**9, bytes_accessed=4 * 2**20, transcendentals=0),
        name="output",
    )(my_tensor.reshape(1).astype(jnp.int32), gathered, full_weight, cand_rows)
    placed = lax.all_to_all(mixed, "tensor", split_axis=0, concat_axis=0, tiled=True)
    return placed.reshape(row_count, out_width)


def solution(mesh):
    in_specs = (
        P("shard", None),
        P(None, None, "tensor"),
        P("tensor", None),
        P("tensor"),
        P("shard", None, None, "tensor"),
        P(),
        P("shard", None),
        P(),
    )
    out_specs = P("shard", "tensor")
    return jax.shard_map(body, mesh=mesh, in_specs=in_specs, out_specs=out_specs, check_vma=False)
```

time: 356 us -> 169 us (0.47)
  waiting for transfers between devices: 152 us -> 31.6 us
  local copies, waits for them, and re-layouts: 90 us -> 25.7 us
  Pallas kernels: 0 us -> 56.3 us
  matrix products: 44.8 us -> 0 us
  other arithmetic: 33.6 us -> 0.26 us
  blocking collectives: 0 us -> 20.2 us
  starting transfers between devices: 17 us -> 20.8 us
    reduce_scatter x1 -> x0, waiting for transfers between devices: 94.3 us -> none  [body(): lax.psum_scatter(partial_sum, 'tensor', scatter_dimension=1, tiled=True)]
    pallas_call x0 -> x5, Pallas kernels: none -> 56.3 us  [the longest x1 29.1 us: body(): pl.pallas_call(attend_kernel, in_specs=[pl.BlockSpec(memory_space=pltpu.S...]
    dot_general x10 -> x0, matrix products: 44.8 us -> none  [the longest x8 34.9 us: add_block(): jnp.einsum('jbu,ubl->jbl', weight_matrices, history_value_rows, preferred...]
    ppermute x1 -> x0, waiting for transfers between devices: 42.6 us -> none  [partner(): lax.ppermute(array, axis, [(i, i ^ 1 << apart) for i in range(lax.axis_si...]
    all_to_all x0 -> x1, blocking collectives: none -> 20.2 us  [body(): lax.all_to_all(mixed, 'tensor', split_axis=0, concat_axis=0, tiled=True)]
    another operation x4 -> x0, other arithmetic: 20.2 us -> none
    another operation x7 -> x0, local copies, waits for them, and re-layouts: 17.4 us -> none  [the longest x2 11.1 us: attend_rows(): pieces = packet.reshape(row_count, 3, head_count, DH)]
    all_to_all x2 -> x3, waiting for transfers between devices: 15.5 us -> 30.9 us  [the longest x1 18 us: body(): lax.all_to_all(hidden.reshape(tensor_count, owned, width), 'tensor', spli...]
  transfers between devices with their start and end apart: 4 -> 4, of which waited for: 3 -> 3; matrix products, arithmetic and copies ran while one was open for 6% -> 7% of each run, Pallas kernels for 0% -> 26%
where the time goes in v1:
time: 169 us; the launch traced here: 168 us
  Pallas kernels  56.3 us (33%)
  waiting for transfers between devices  31.6 us (19%)
  local copies, waits for them, and re-layouts  25.7 us (15%)
  starting transfers between devices  20.8 us (12%)
  blocking collectives  20.2 us (12%)
  between operations  13.6 us (8%)
    pallas_call x1, Pallas kernels, body(): pl.pallas_call(attend_kernel, in_specs=[pl.BlockSpec(memory_space=pltpu.S...  29.1 us
    all_to_all x1, blocking collectives, body(): lax.all_to_all(mixed, 'tensor', split_axis=0, concat_axis=0, tiled=True)  20.2 us
    all_to_all x1, waiting for transfers between devices, body(): lax.all_to_all(hidden.reshape(tensor_count, owned, width), 'tensor', spli...  18 us
    unnamed x31, local copies, waits for them, and re-layouts  15.4 us
    pallas_call x1, Pallas kernels, body(): pl.pallas_call(functools.partial(query_kernel, capacity), grid=(steps,),...  10.1 us
    all_to_all x1, starting transfers between devices, body(): lax.all_to_all(sent.reshape(shard_count, slot_count * capacity, width), '...  8.72 us
    all_to_all x1, starting transfers between devices, body(): lax.all_to_all(hidden.reshape(tensor_count, owned, width), 'tensor', spli...  8.18 us
    all_to_all x1, waiting for transfers between devices, body(): lax.all_to_all(answered.reshape(shard_count, slot_count * capacity, width...  7.39 us
  transfers between devices with their start and end apart: 4, of which 3 were waited for; matrix products, arithmetic and copies ran while one was open for 7% of the time, Pallas kernels for 26%

profile of v1, /device:TPU:1, one launch (start us, length us, event | category | flops | bytes accessed | tf_op | source)
XLA Modules:
  0.0 168.4 jit_solution(1473536337699873282)
XLA Ops:
  6.5 0.0 copy-start.12
  6.5 0.0 copy-start.3
  6.5 5.3 %fusion.1 = (bf16[1024,1,128]{2,1,0:T(2,128)(2,1)S(1)}, bf16[1024,1,128]{2,1,0:T(2,128)(2,1)}, bf16[1024,1,128]{2,1,0:T(2,128)(2,1)S(1)}, bf16[1024,1,128]{2,1,0:T(2,128)(2,1)}) fusion(bf16[1024,4,128]{2,1,0:T(4,128)(2,1)} %param.9), kind=kLoop, calls=%fused_computation.11 | loop fusion | bytes 2097152 | tf_op jit(solution)/shard_map/slice | solution.py:217
  11.9 0.0 copy-done.12
  11.9 0.1 fusion.2
  12.0 0.1 add_add_fusion
  12.0 0.1 add_select_fusion
  12.1 0.1 select_n.20.source_ref
  12.2 0.1 copy_bitcast_fusion.3
  12.3 0.0 copy-done.3
  12.3 0.0 copy-start
  12.3 2.2 %copy-done = bf16[2048,1024]{1,0:T(8,128)(2,1)S(1)} copy-done((bf16[2048,1024]{1,0:T(8,128)(2,1)S(1)}, bf16[2048,1024]{1,0:T(8,128)(2,1)}, u32[]{:S(2)}) %copy-start) | copy-done | bytes 4194328
  14.5 10.1 %query.1 = (bf16[4096,128]{1,0:T(8,128)(2,1)}, bf16[2048,128]{1,0:T(8,128)(2,1)S(1)}, s32[1,2048]{1,0:T(1,128)S(1)}) custom-call(bf16[2048,1024]{1,0:T(8,128)(2,1)S(1)} %copy-done, bf16[1024,128]{1,0:T(8,128)(2,1)S(1)} %get-tuple-element.26.weight_ref, s32[1,2048]{1,0:T(1,128)S(1)} %bitcast.29, s32[64,1]{1,0:T(8,128)S(1)} %select_n.20.source_ref), custom_call_target="tpu_custom_call" | custom-call | flops 4000000000 | bytes 6291456 | tf_op jit(solution)/shard_map/query/pallas_call | solution.py:184
  24.5 0.0 copy-start.5
  24.6 0.9 copy-done.5
  25.4 0.0 copy-start.9
  25.4 8.7 %all-to-all-start = ((bf16[32,128,128]{2,1,0:T(8,128)(2,1)}), bf16[32,128,128]{2,1,0:T(8,128)(2,1)S(1)}, u32[]{:S(2)}, u32[]{:S(2)}) async-start(bf16[32,128,128]{2,1,0:T(8,128)(2,1)} %bitcast.4), calls=%async_computation | async-start | bytes 2097152 | tf_op jit(solution)/shard_map/all_to_all | solution.py:213
  34.1 0.0 all-gather.2.cloned.1.call-start
  34.2 0.7 all-gather.2.cloned.1.call-update
  34.9 0.0 copy-done.9
  34.9 4.2 %fusion = (bf16[2,2048,1,128]{3,2,1,0:T(2,128)(2,1)}, bf16[2,2048,1,128]{3,2,1,0:T(2,128)(2,1)}) fusion(bf16[2,2048,2,128]{3,2,1,0:T(2,128)(2,1)S(1)} %copy-done.9), kind=kLoop, calls=%fused_computation.10 | loop fusion | bytes 4194304 | tf_op jit(solution)/shard_map/slice | solution.py:235
  39.1 1.7 %copy.35 = bf16[2,2048,1,128]{3,1,0,2:T(8,128)(2,1)S(1)} copy(bf16[2,2048,1,128]{3,2,1,0:T(2,128)(2,1)} %get-tuple-element.15) | data formatting | bytes 2097152
  40.9 0.0 copy-start.13
  40.9 4.6 %copy.25 = bf16[2,2048,1,128]{1,3,0,2:T(8,128)(2,1)S(1)} copy(bf16[2,2048,1,128]{3,2,1,0:T(2,128)(2,1)} %get-tuple-element.16) | data formatting | bytes 2097152
  45.4 0.0 copy-done.13
  45.4 0.1 dynamic_slice.3.length_ref
  45.5 5.5 %all-to-all-done = bf16[32,128,128]{2,1,0:T(8,128)(2,1)S(1)} async-done(((bf16[32,128,128]{2,1,0:T(8,128)(2,1)}), bf16[32,128,128]{2,1,0:T(8,128)(2,1)S(1)}, u32[]{:S(2)}, u32[]{:S(2)}) %all-to-all-start) | async-done | bytes 1048608 | tf_op jit(solution)/shard_map/all_to_all | solution.py:213
  51.0 29.1 %attend.1 = bf16[32,2,64,128]{3,2,1,0:T(8,128)(2,1)S(1)} custom-call(s32[2]{0:T(128)S(1)} %dynamic_slice.3.length_ref, bf16[32,2,64,128]{3,2,1,0:T(8,128)(2,1)S(1)} %bitcast.25, bf16[2,128,2048]{2,1,0:T(8,128)(2,1)S(1)} %bitcast.24, bf16[2,2048,128]{2,1,0:T(8,128)(2,1)S(1)} %bitcast.23), custom_call_target="tpu_custom_call" | custom-call | flops 12000000000 | bytes 4194304 | tf_op jit(solution)/shard_map/attend/pallas_call | solution.py:239
  80.1 0.0 copy-start.2
  80.1 1.0 copy-done.2
  81.1 0.0 copy-start.10
  81.1 0.0 copy-start.11
  81.1 3.8 %all-to-all-start.1 = ((bf16[32,128,128]{2,1,0:T(8,128)(2,1)}), bf16[32,128,128]{2,1,0:T(8,128)(2,1)S(1)}, u32[]{:S(2)}, u32[]{:S(2)}) async-start(bf16[32,128,128]{2,1,0:T(8,128)(2,1)} %bitcast.27), calls=%async_computation.1 | async-start | bytes 2097152 | tf_op jit(solution)/shard_map/all_to_all | solution.py:250
  85.0 0.0 copy-start.4
  85.0 0.4 copy.23.key_ref
  85.4 0.0 copy-start.6
  85.4 0.0 copy-done.10
  85.4 0.0 copy-done.11
  85.4 0.1 copy_bitcast_fusion.1
  85.5 0.1 pad_maximum_fusion.weight_ref
  85.6 0.1 copy-done.4
  85.6 0.8 copy-done.6
  86.4 7.2 %side.1 = (bf16[2048,128]{1,0:T(8,128)(2,1)S(1)}, f32[2048,128]{1,0:T(8,128)S(1)}) custom-call(bf16[2048,1024]{1,0:T(8,128)(2,1)} %residual_ref.1, bf16[1024,384]{1,0:T(8,128)(2,1)S(1)} %pad_maximum_fusion.weight_ref, bf16[2048,128]{1,0:T(8,128)(2,1)S(1)} %copy-done.6, f32[2]{0:T(128)S(1)} %copy-done.4), custom_call_target="tpu_custom_call" | custom-call | flops 4000000000 | bytes 6291456 | tf_op jit(solution)/shard_map/side/pallas_call | solution.py:218
  93.6 0.0 copy-start.7
  93.7 0.8 copy-done.7
  94.4 7.4 %all-to-all-done.1 = bf16[32,128,128]{2,1,0:T(8,128)(2,1)S(1)} async-done(((bf16[32,128,128]{2,1,0:T(8,128)(2,1)}), bf16[32,128,128]{2,1,0:T(8,128)(2,1)S(1)}, u32[]{:S(2)}, u32[]{:S(2)}) %all-to-all-start.1) | async-done | bytes 1048608 | tf_op jit(solution)/shard_map/all_to_all | solution.py:250
  101.8 0.0 copy-start.8
  101.8 1.0 copy-done.8
  102.9 6.9 %hidden.1 = bf16[2048,128]{1,0:T(8,128)(2,1)} custom-call(s32[2048,1]{1,0:T(8,128)S(1)} %copy.23.key_ref, bf16[4096,128]{1,0:T(8,128)(2,1)S(1)} %bitcast.26, f32[2048,128]{1,0:T(8,128)S(1)} %get-tuple-element.13.self_ref, bf16[2048,128]{1,0:T(8,128)(2,1)S(1)} %copy-done.8), custom_call_target="tpu_custom_call" | custom-call | flops 4000000000 | bytes 4194304 | tf_op jit(solution)/shard_map/hidden/pallas_call | solution.py:255
  109.8 8.2 %all-to-all-start.2 = ((bf16[8,256,128]{2,1,0:T(8,128)(2,1)}), bf16[8,256,128]{2,1,0:T(8,128)(2,1)S(1)}, u32[]{:S(2)}, u32[]{:S(2)}) async-start(bf16[8,256,128]{2,1,0:T(8,128)(2,1)} %bitcast.14), calls=%async_computation.2 | async-start | bytes 1048576 | tf_op jit(solution)/shard_map/all_to_all | solution.py:272
  118.0 18.0 %all-to-all-done.2.hidden_ref = bf16[8,256,128]{2,1,0:T(8,128)(2,1)S(1)} async-done(((bf16[8,256,128]{2,1,0:T(8,128)(2,1)}), bf16[8,256,128]{2,1,0:T(8,128)(2,1)S(1)}, u32[]{:S(2)}, u32[]{:S(2)}) %all-to-all-start.2) | async-done | bytes 524320 | tf_op jit(solution)/shard_map/all_to_all | solution.py:272
  135.9 0.0 all-gather.2.cloned.1.call-done.weight_ref
  135.9 0.0 copy-start.1
  135.9 1.6 copy-done.1
  137.5 3.0 %output.1 = bf16[8,256,128]{2,1,0:T(8,128)(2,1)S(1)} custom-call(s32[1]{0:T(128)} %bitcast.place_ref, bf16[8,256,128]{2,1,0:T(8,128)(2,1)S(1)} %all-to-all-done.2.hidden_ref, bf16[1024,1024]{1,0:T(8,128)(2,1)S(1)} %copy-done.1, bf16[2048,1024]{1,0:T(8,128)(2,1)} %residual_ref.1), custom_call_target="tpu_custom_call" | custom-call | flops 1000000000 | bytes 4194304 | tf_op jit(solution)/shard_map/output/pallas_call | solution.py:276
  140.5 20.2 %all_to_all.20 = bf16[8,256,128]{2,1,0:T(8,128)(2,1)S(1)} all-to-all(bf16[8,256,128]{2,1,0:T(8,128)(2,1)S(1)} %output.1), channel_id=1, replica_groups=mesh['shard'=32,'tensor'=8] {'tensor'}, dimensions={0} | all-to-all | bytes 1048576 | tf_op jit(solution)/shard_map/all_to_all | solution.py:293
  160.8 0.8 copy.37
Async XLA Ops:
  6.5 5.4 %copy-start.12 = (s32[32]{0:T(128)S(1)}, s32[32]{0:T(128)}, u32[]{:S(2)}) copy-start(s32[32]{0:T(128)} %param.15) | copy-start | bytes 388
  6.5 5.7 %copy-start.3 = (s32[2048,1]{0,1:T(1,128)S(1)}, s32[2048,1]{0,1:T(1,128)}, u32[]{:S(2)}) copy-start(s32[2048,1]{0,1:T(1,128)} %param.14) | copy-start | bytes 24580
  12.3 2.2 %copy-start = (bf16[2048,1024]{1,0:T(8,128)(2,1)S(1)}, bf16[2048,1024]{1,0:T(8,128)(2,1)}, u32[]{:S(2)}) copy-start(bf16[2048,1024]{1,0:T(8,128)(2,1)} %residual_ref.1) | copy-start | bytes 12582916
  24.5 0.9 copy-start.5
  25.4 9.5 %copy-start.9 = (bf16[2,2048,2,128]{3,2,1,0:T(2,128)(2,1)S(1)}, bf16[2,2048,2,128]{3,2,1,0:T(2,128)(2,1)}, u32[]{:S(2)}) copy-start(bf16[2,2048,2,128]{3,2,1,0:T(2,128)(2,1)} %param.12) | copy-start | bytes 6291460
  25.4 25.6 %all-to-all-start = ((bf16[32,128,128]{2,1,0:T(8,128)(2,1)}), bf16[32,128,128]{2,1,0:T(8,128)(2,1)S(1)}, u32[]{:S(2)}, u32[]{:S(2)}) async-start(bf16[32,128,128]{2,1,0:T(8,128)(2,1)} %bitcast.4), calls=%async_computation | async-start | bytes 2097152 | tf_op jit(solution)/shard_map/all_to_all | solution.py:213
  34.1 101.8 %all-gather.2.cloned.1.call-start = ((), (), s32[]{:S(2)}) async-start(), calls=%async_computation.4 | async-start | bytes 2359296 | tf_op jit(solution)/shard_map/all_gather | solution.py:180
  40.9 4.6 %copy-start.13 = (s32[64]{0:T(128)S(1)}, s32[64]{0:T(128)}, u32[]{:S(2)}) copy-start(s32[64]{0:T(128)} %param.13) | copy-start | bytes 772
  80.1 1.0 copy-start.2
  81.1 4.3 %copy-start.10 = (bf16[1024,1,128]{2,1,0:T(2,128)(2,1)S(1)}, bf16[1024,1,128]{2,1,0:T(2,128)(2,1)}, u32[]{:S(2)}) copy-start(bf16[1024,1,128]{2,1,0:T(2,128)(2,1)} %get-tuple-element.18) | copy-start | bytes 786436
  81.1 4.3 %copy-start.11 = (bf16[1024,1,128]{2,1,0:T(2,128)(2,1)S(1)}, bf16[1024,1,128]{2,1,0:T(2,128)(2,1)}, u32[]{:S(2)}) copy-start(bf16[1024,1,128]{2,1,0:T(2,128)(2,1)} %get-tuple-element.20) | copy-start | bytes 786436
  81.1 20.7 %all-to-all-start.1 = ((bf16[32,128,128]{2,1,0:T(8,128)(2,1)}), bf16[32,128,128]{2,1,0:T(8,128)(2,1)S(1)}, u32[]{:S(2)}, u32[]{:S(2)}) async-start(bf16[32,128,128]{2,1,0:T(8,128)(2,1)} %bitcast.27), calls=%async_computation.1 | async-start | bytes 2097152 | tf_op jit(solution)/shard_map/all_to_all | solution.py:250
  85.0 0.7 copy-start.4
  85.4 1.0 copy-start.6
  93.6 0.8 copy-start.7
  101.8 1.0 copy-start.8
  109.8 26.1 %all-to-all-start.2 = ((bf16[8,256,128]{2,1,0:T(8,128)(2,1)}), bf16[8,256,128]{2,1,0:T(8,128)(2,1)S(1)}, u32[]{:S(2)}, u32[]{:S(2)}) async-start(bf16[8,256,128]{2,1,0:T(8,128)(2,1)} %bitcast.14), calls=%async_computation.2 | async-start | bytes 1048576 | tf_op jit(solution)/shard_map/all_to_all | solution.py:272
  135.9 1.6 copy-start.1
Sparse Core Ops, SparseCore 0:
  36.8 40.0 all-gather.1
